TPU v7x, 32 devices: a whole 2x2x4 slice. The times are simulated.
32 devices in a mesh: ax: 16 (over z, y, x), rad: 2 (over core).
Axes of the slice: x: 2, y: 2, z: 4, core: 2. Of those that a mesh axis runs over, the one named last changes fastest.
Arguments:
- fields: float32 [128, 5, 8, 1024], P('ax', None, None, 'rad'), may hold values from -6 to 6
Outputs:
- axial_deriv: float32 [128, 5, 8, 1024], P('ax', None, None, 'rad')
- filtered: float32 [128, 5, 8, 1024], P('ax', None, None, 'rad')
- radial_deriv: float32 [128, 5, 8, 1024], P('ax', None, None, 'rad')
All inputs are finite; a program needn't handle non-finite values.
Results may differ from a plain program's by a relative error of at most 0.0003.
Values sent between devices are 32-bit elements; how exact they have to be, the bound alone decides.
A program may use at most 128 MiB of HBM per device.

v0:
```python
import jax
import jax.numpy as jnp
from jax import lax
from jax.sharding import PartitionSpec as P

deriv_alpha = 1.0 / 3.0
filter_alpha = 0.4999
block_rows = 64


def with_halo(array, sides, width):
    for axis, dim in sides:
        size, length = (lax.axis_size(axis), array.shape[dim])
        up = [(i, (i + 1) % size) for i in range(size - 1)]
        down = [(j, i) for i, j in up]
        last = lax.slice_in_dim(array, length - width, length, axis=dim)
        initial = lax.slice_in_dim(array, 0, width, axis=dim)
        before = lax.ppermute(last, axis, up)
        after = lax.ppermute(initial, axis, down)
        array = jnp.concatenate([before, array, after], axis=dim)
    return array


def filter_weights():
    return [
        (93.0 + 70.0 * filter_alpha) / 128.0,
        (7.0 + 18.0 * filter_alpha) / 16.0,
        (-7.0 + 14.0 * filter_alpha) / 32.0,
        (1.0 - 2.0 * filter_alpha) / 16.0,
        (-1.0 + 2.0 * filter_alpha) / 128.0,
    ]


def sources(padded, count):

    def shifted(k):
        return padded[4 + k : 4 + k + count]

    deriv_rhs = 7.0 / 9.0 * (shifted(1) - shifted(-1)) + 1.0 / 36.0 * (shifted(2) - shifted(-2))
    weights = filter_weights()
    filter_rhs = weights[0] * shifted(0)
    for n in range(1, 5):
        filter_rhs = filter_rhs + weights[n] / 2.0 * (shifted(n) + shifted(-n))
    return jnp.stack([deriv_rhs, filter_rhs])


def pivots(alpha, rows):
    root = (1.0 - 4.0 * alpha * alpha) ** 0.5
    big_root = (1.0 + root) / 2.0
    ratio = (1.0 - root) / (1.0 + root)
    return big_root * (1.0 - jnp.power(ratio, rows + 2.0)) / (1.0 - jnp.power(ratio, rows + 1.0))


def tables(alpha, rows):
    length = rows.shape[-1]
    piv = pivots(alpha, rows)
    before = pivots(alpha, jnp.maximum(rows - 1.0, 0.0))
    log_fwd = jnp.log(alpha / before)
    cum_fwd = jnp.cumsum(log_fwd, axis=-1)
    log_bwd = jnp.log(alpha / piv)
    cum_bwd = jnp.cumsum(log_bwd, axis=-1)
    excl_bwd = cum_bwd - log_bwd
    index = jnp.arange(length)
    parity = ((index[:, None] - index[None, :]) % 2).astype(jnp.float32)
    signs = 1.0 - 2.0 * parity
    lower = index[:, None] >= index[None, :]
    upper = index[:, None] <= index[None, :]
    diff_fwd = jnp.minimum(cum_fwd[..., :, None] - cum_fwd[..., None, :], 0.0)
    forward = jnp.where(lower, signs * jnp.exp(diff_fwd), 0.0)
    diff_bwd = jnp.minimum(excl_bwd[..., None, :] - excl_bwd[..., :, None], 0.0)
    backward = jnp.where(upper, signs * jnp.exp(diff_bwd) / piv[..., None, :], 0.0)
    sign_in = 1.0 - 2.0 * ((index + 1) % 2).astype(jnp.float32)
    gain_in = sign_in * jnp.exp(cum_fwd)
    sign_out = 1.0 - 2.0 * ((length - index) % 2).astype(jnp.float32)
    gain_out = sign_out * jnp.exp(cum_bwd[..., length - 1 :] - excl_bwd)
    return (forward, gain_in, backward, gain_out)


def combine(earlier, later):
    return (earlier[0] * later[0], later[1] + later[0] * earlier[1])


def solve(rhs, rows, chain_forward, chain_backward):
    parts = [tables(deriv_alpha, rows), tables(filter_alpha, rows)]
    forward = jnp.stack([parts[0][0], parts[1][0]])
    gain_in = jnp.stack([parts[0][1], parts[1][1]])
    backward = jnp.stack([parts[0][2], parts[1][2]])
    gain_out = jnp.stack([parts[0][3], parts[1][3]])
    local_fwd = jnp.einsum("sbkj,sbjl->sbkl", forward, rhs, precision=lax.Precision.HIGHEST)
    incoming = chain_forward(gain_in[:, :, -1:], local_fwd[:, :, -1, :])
    eliminated = local_fwd + gain_in[..., None] * incoming[:, :, None, :]
    local_bwd = jnp.einsum("sbkj,sbjl->sbkl", backward, eliminated, precision=lax.Precision.HIGHEST)
    outgoing = chain_backward(gain_out[:, :, :1], local_bwd[:, :, 0, :])
    return local_bwd + gain_out[..., None] * outgoing[:, :, None, :]


def block_chain(coeff, offset):
    inclusive = lax.associative_scan(combine, (coeff, offset), axis=1)
    return jnp.concatenate([jnp.zeros_like(offset[:, :1]), inclusive[1][:, :-1]], axis=1)


def block_forward(coeff, offset):
    return block_chain(coeff, offset)


def block_backward(coeff, offset):
    flipped = block_chain(jnp.flip(coeff, axis=1), jnp.flip(offset, axis=1))
    return jnp.flip(flipped, axis=1)


def body(fields):
    rows_dev, count, planes, radial = fields.shape
    width = count * planes * radial
    rimmed = with_halo(fields, (("rad", 3),), 3)

    def radial_cell(k):
        return rimmed[:, :, :, 3 + k : 3 + k + radial]

    radial_deriv = (
        45.0 * (radial_cell(1) - radial_cell(-1))
        - 9.0 * (radial_cell(2) - radial_cell(-2))
        + (radial_cell(3) - radial_cell(-3))
    ) / 60.0
    flat = fields.reshape(rows_dev, width)
    lines = lax.all_to_all(flat, "ax", split_axis=1, concat_axis=0, tiled=True)
    total = lines.shape[0]
    padded = jnp.pad(lines, ((4, 4), (0, 0)))
    rhs = sources(padded, total)
    blocks = total // block_rows
    rows = jnp.arange(total, dtype=jnp.float32).reshape(blocks, block_rows)
    solved = solve(rhs.reshape(2, blocks, block_rows, -1), rows, block_forward, block_backward)
    solved = solved.reshape(2, total, -1)
    result = lax.all_to_all(solved, "ax", split_axis=1, concat_axis=2, tiled=True)
    axial_deriv = result[0].reshape(fields.shape)
    filtered = result[1].reshape(fields.shape)
    return (axial_deriv, filtered, radial_deriv)


def solution(mesh):
    in_specs = (P("ax", None, None, "rad"),)
    out_specs = (P("ax", None, None, "rad"), P("ax", None, None, "rad"), P("ax", None, None, "rad"))
    return jax.shard_map(body, mesh=mesh, in_specs=in_specs, out_specs=out_specs, check_vma=False)
```

profile of v0, /device:TPU:8, one launch (start us, length us, event | category | flops | bytes accessed | tf_op | source)
XLA Modules:
  0.0 72.5 jit_solution(13071631974729192661)
XLA Ops:
  0.6 1.3 %all_to_all.25 = f32[8,16,1280]{2,1,0:T(8,128)S(1)} reshape(f32[8,5,8,512]{3,2,1,0:T(8,128)} %param.1) | data formatting | bytes 1310720 | tf_op jit(solution)/shard_map/all_to_all | solution.py:125
  1.9 1.2 %copy.11 = f32[8,16,1280]{2,0,1:T(8,128)} copy(f32[8,16,1280]{2,1,0:T(8,128)S(1)} %all_to_all.25) | data formatting | bytes 1310720 | tf_op jit(solution)/shard_map/all_to_all | solution.py:125
  3.2 7.2 %all-to-all-start = ((f32[8,16,1280]{2,0,1:T(8,128)}), f32[8,16,1280]{2,0,1:T(8,128)S(1)}, u32[]{:S(2)}, u32[]{:S(2)}) async-start(f32[8,16,1280]{2,0,1:T(8,128)} %copy.11), calls=%async_computation | async-start | bytes 1310720 | tf_op jit(solution)/shard_map/all_to_all | solution.py:125
  10.5 0.2 reduce_window_sum.36
  10.8 0.2 reduce_window_sum.29
  11.0 0.2 reduce_window_sum.28
  11.3 0.2 reduce_window_sum.27
  11.5 0.2 slice_reduce_fusion
  12.4 15.2 %all-to-all-done = f32[8,16,1280]{2,0,1:T(8,128)S(1)} async-done(((f32[8,16,1280]{2,0,1:T(8,128)}), f32[8,16,1280]{2,0,1:T(8,128)S(1)}, u32[]{:S(2)}, u32[]{:S(2)}) %all-to-all-start) | async-done | bytes 655392 | tf_op jit(solution)/shard_map/all_to_all | solution.py:125
  27.6 0.7 multiply_add_fusion.2
  28.3 1.2 %fusion = f32[2,2,64,1280]{3,2,1,0:T(8,128)S(1)} fusion(f32[1,2,64,1280]{3,2,1,0:T(8,128)S(1)} %bitcast.45, f32[1,2,64,1280]{3,2,1,0:T(8,128)S(1)} %bitcast.44, f32[1,2,64,64]{3,2,1,0:T(8,128)S(1)} %get-tuple-element.13, f32[1,2,64,64]{3,2,1,0:T(8,128)S(1)} %get-tuple-element.14), kind=kOutput, calls=%fused_computation | convolution fusion | flops 252002304 | bytes 2686976 | tf_op jit(solution)/shard_map/sbkj,sbjl->sbkl/dot_general | solution.py:89
  29.7 1.3 %fusion.4 = f32[2,2,64,1280]{3,2,1,0:T(8,128)S(1)} fusion(f32[2,2,64,1280]{3,2,1,0:T(8,128)S(1)} %fusion, f32[2,2,1280]{2,1,0:T(2,128)S(1)} %concatenate.18, f32[2,2,64]{2,1,0:T(2,128)S(1)} %pad_maximum_fusion.1, f32[1,2,64,64]{3,2,1,0:T(8,128)S(1)} %get-tuple-element.10, f32[1,2,64,64]{3,2,1,0:T(8,128)S(1)} %get-tuple-element.9), kind=kOutput, calls=%fused_computation.5 | convolution fusion | flops 252329984 | bytes 2708480 | tf_op jit(solution)/shard_map/sbkj,sbjl->sbkl/dot_general | solution.py:92
  31.2 0.3 rev.7
  31.6 2.1 %copy.12 = f32[2,128,1280]{2,0,1:T(2,128)} copy(f32[2,128,1280]{2,1,0:T(8,128)S(1)} %bitcast.42) | data formatting | bytes 2621440 | tf_op jit(solution)/shard_map/reshape | solution.py:132
  33.7 4.8 %all-to-all-start.1 = ((f32[2,128,1280]{2,0,1:T(2,128)}), f32[2,128,1280]{2,0,1:T(2,128)S(1)}, u32[]{:S(2)}, u32[]{:S(2)}) async-start(f32[2,128,1280]{2,0,1:T(2,128)} %copy.12), calls=%async_computation.1 | async-start | bytes 2621440 | tf_op jit(solution)/shard_map/all_to_all | solution.py:133
  38.6 1.3 %collective-permute-start = (f32[8,5,8,3]{3,2,1,0:T(8,128)S(1)}, f32[8,5,8,3]{3,2,1,0:T(8,128)S(1)}, u32[]{:S(2)}, u32[]{:S(2)}) collective-permute-start(f32[8,5,8,3]{3,2,1,0:T(8,128)S(1)} %get-tuple-element.5), channel_id=1, source_target_pairs={{1,0},{3,2},{5,4},{7,6},{9,8},{11,10},{13,12},{15,14},{17,16},{19,... | collective-permute-start | bytes 11528 | tf_op jit(solution)/shard_map/ppermute | solution.py:19
  39.9 3.0 %collective-permute-start.1 = (f32[8,5,8,3]{3,2,1,0:T(8,128)S(1)}, f32[8,5,8,3]{3,2,1,0:T(8,128)S(1)}, u32[]{:S(2)}, u32[]{:S(2)}) collective-permute-start(f32[8,5,8,3]{3,2,1,0:T(8,128)S(1)} %get-tuple-element.6), channel_id=1, source_target_pairs={{0,1},{2,3},{4,5},{6,7},{8,9},{10,11},{12,13},{14,15},{16,17},{18,... | collective-permute-start | bytes 11528 | tf_op jit(solution)/shard_map/ppermute | solution.py:18
  43.0 0.9 %collective-permute-done.1 = f32[8,5,8,3]{3,2,1,0:T(8,128)S(1)} collective-permute-done((f32[8,5,8,3]{3,2,1,0:T(8,128)S(1)}, f32[8,5,8,3]{3,2,1,0:T(8,128)S(1)}, u32[]{:S(2)}, u32[]{:S(2)}) %collective-permute-start.1) | collective-permute-done | bytes 3872 | tf_op jit(solution)/shard_map/ppermute | solution.py:18
  44.0 2.0 %fusion.12 = f32[8,5,8,512]{3,2,1,0:T(8,128)} fusion(f32[8,5,8,512]{3,2,1,0:T(8,128)S(1)} %copy-done, f32[8,5,8,3]{3,2,1,0:T(8,128)S(1)} %collective-permute-done.1, f32[8,5,8,515]{3,2,1,0:T(8,128)S(1)} %constant_dynamic-update-slice_fusion), kind=kLoop, calls=%fused_computation.17 | loop fusion | flops 1802240 | bytes 3280640 | tf_op jit(solution)/shard_map/div | solution.py:119
  46.0 23.0 %all-to-all-done.1 = f32[2,128,1280]{2,0,1:T(2,128)S(1)} async-done(((f32[2,128,1280]{2,0,1:T(2,128)}), f32[2,128,1280]{2,0,1:T(2,128)S(1)}, u32[]{:S(2)}, u32[]{:S(2)}) %all-to-all-start.1) | async-done | bytes 1310752 | tf_op jit(solution)/shard_map/all_to_all | solution.py:133
  69.0 1.0 %fusion.64 = (f32[1,8,16,1280]{3,0,1,2:T(1,128)S(1)}, f32[1,8,16,1280]{3,0,1,2:T(1,128)S(1)}) fusion(f32[2,8,16,1280]{3,0,1,2:T(2,128)S(1)} %bitcast.41), kind=kLoop, calls=%fused_computation.122 | loop fusion | bytes 2621440 | tf_op jit(solution)/shard_map/slice | solution.py:135
  70.0 0.2 copy.14
  70.3 1.0 %reshape_squeeze.7 = f32[8,5,8,512]{3,2,1,0:T(8,128)} reshape(f32[1,8,16,1280]{3,2,1,0:T(8,128)S(1)} %copy.14) | data formatting | bytes 1310720 | tf_op jit(solution)/shard_map/reshape;squeeze | solution.py:135
  71.5 1.0 %reshape_squeeze.6 = f32[8,5,8,512]{3,2,1,0:T(8,128)} reshape(f32[1,8,16,1280]{3,2,1,0:T(8,128)S(1)} %copy.13) | data formatting | bytes 1310720 | tf_op jit(solution)/shard_map/reshape;squeeze | solution.py:134
  (35 shorter events, 1.6 us)
Async XLA Ops:
  3.2 24.4 %all-to-all-start = ((f32[8,16,1280]{2,0,1:T(8,128)}), f32[8,16,1280]{2,0,1:T(8,128)S(1)}, u32[]{:S(2)}, u32[]{:S(2)}) async-start(f32[8,16,1280]{2,0,1:T(8,128)} %copy.11), calls=%async_computation | async-start | bytes 1310720 | tf_op jit(solution)/shard_map/all_to_all | solution.py:125
  33.7 4.8 %copy-start = (f32[8,5,8,512]{3,2,1,0:T(8,128)S(1)}, f32[8,5,8,512]{3,2,1,0:T(8,128)}, u32[]{:S(2)}) copy-start(f32[8,5,8,512]{3,2,1,0:T(8,128)} %param.1) | copy-start | bytes 1966084
  33.7 35.3 %all-to-all-start.1 = ((f32[2,128,1280]{2,0,1:T(2,128)}), f32[2,128,1280]{2,0,1:T(2,128)S(1)}, u32[]{:S(2)}, u32[]{:S(2)}) async-start(f32[2,128,1280]{2,0,1:T(2,128)} %copy.12), calls=%async_computation.1 | async-start | bytes 2621440 | tf_op jit(solution)/shard_map/all_to_all | solution.py:133
  38.6 4.4 %collective-permute-start = (f32[8,5,8,3]{3,2,1,0:T(8,128)S(1)}, f32[8,5,8,3]{3,2,1,0:T(8,128)S(1)}, u32[]{:S(2)}, u32[]{:S(2)}) collective-permute-start(f32[8,5,8,3]{3,2,1,0:T(8,128)S(1)} %get-tuple-element.5), channel_id=1, source_target_pairs={{1,0},{3,2},{5,4},{7,6},{9,8},{11,10},{13,12},{15,14},{17,16},{19,... | collective-permute-start | bytes 11528 | tf_op jit(solution)/shard_map/ppermute | solution.py:19
  39.9 4.1 %collective-permute-start.1 = (f32[8,5,8,3]{3,2,1,0:T(8,128)S(1)}, f32[8,5,8,3]{3,2,1,0:T(8,128)S(1)}, u32[]{:S(2)}, u32[]{:S(2)}) collective-permute-start(f32[8,5,8,3]{3,2,1,0:T(8,128)S(1)} %get-tuple-element.6), channel_id=1, source_target_pairs={{0,1},{2,3},{4,5},{6,7},{8,9},{10,11},{12,13},{14,15},{16,17},{18,... | collective-permute-start | bytes 11528 | tf_op jit(solution)/shard_map/ppermute | solution.py:18
where the time goes:
time: 72.9 us; the launch traced here: 72.5 us
  waiting for transfers between devices  39.2 us (54%)
  starting transfers between devices  16.3 us (22%)
  local copies, waits for them, and re-layouts  8.85 us (12%)
  other arithmetic  4.78 us (7%)
  matrix products  2.54 us (3%)
  between operations  0.86 us (1%)
    all_to_all x1, waiting for transfers between devices, body(): lax.all_to_all(solved, 'ax', split_axis=1, concat_axis=2, tiled=True)  23 us
    all_to_all x1, waiting for transfers between devices, body(): lines = lax.all_to_all(flat, 'ax', split_axis=1, concat_axis=0, tiled=True)  15.2 us
    all_to_all x1, starting transfers between devices, body(): lines = lax.all_to_all(flat, 'ax', split_axis=1, concat_axis=0, tiled=True)  7.22 us
    all_to_all x1, starting transfers between devices, body(): lax.all_to_all(solved, 'ax', split_axis=1, concat_axis=2, tiled=True)  4.77 us
    ppermute x1, starting transfers between devices, with_halo(): before = lax.ppermute(last, axis, up)  3.05 us
    all_to_all x2, local copies, waits for them, and re-layouts, body(): lines = lax.all_to_all(flat, 'ax', split_axis=1, concat_axis=0, tiled=True)  2.53 us
    reshape x1, local copies, waits for them, and re-layouts, body(): solved = solved.reshape(2, total, -1)  2.07 us
    div x1, other arithmetic, body(): (45.0 * (radial_cell(1) - radial_cell(-1)) - 9.0 * (radial_cell(2) - radi...  2.02 us
  transfers between devices with their start and end apart: 4, of which 3 were waited for; matrix products, arithmetic and copies ran while one was open for 6% of the time, Pallas kernels for 0%

commit v1 on v0

--- a/solution.py
+++ b/solution.py
@@ -6,6 +6,22 @@
 deriv_alpha = 1.0 / 3.0
 filter_alpha = 0.4999
 block_rows = 64
+
+
+def pairwise_exchange(shard, axis, split, join):
+    ways, here = (lax.axis_size(axis), lax.axis_index(axis))
+    width = shard.shape[split] // ways
+    dims = list(shard.shape)
+    dims[split] = width
+    height = dims[join]
+    dims[join] = height * ways
+    full = jnp.zeros(dims, shard.dtype)
+    for mask in range(ways):
+        part = lax.dynamic_slice_in_dim(shard, (here ^ mask) * width, width, axis=split)
+        if mask:
+            part = lax.ppermute(part, axis, [(d, d ^ mask) for d in range(ways)])
+        full = lax.dynamic_update_slice_in_dim(full, part, (here ^ mask) * height, axis=join)
+    return full
 
 
 def with_halo(array, sides, width):
@@ -122,7 +138,7 @@
         + (radial_cell(3) - radial_cell(-3))
     ) / 60.0
     flat = fields.reshape(rows_dev, width)
-    lines = lax.all_to_all(flat, "ax", split_axis=1, concat_axis=0, tiled=True)
+    lines = pairwise_exchange(flat, "ax", 1, 0)
     total = lines.shape[0]
     padded = jnp.pad(lines, ((4, 4), (0, 0)))
     rhs = sources(padded, total)

time: 72.9 us -> 106 us (1.45); the launches traced: 72.5 us -> 105 us
  starting transfers between devices: 16.3 us -> 52.9 us
  waiting for transfers between devices: 39.2 us -> 35 us
    ppermute x0 -> x15, starting transfers between devices: none -> 41.4 us  [pairwise_exchange(): part = lax.ppermute(part, axis, [(d, d ^ mask) for d in range(ways)])]
    ppermute x0 -> x15, waiting for transfers between devices: none -> 22.3 us  [pairwise_exchange(): part = lax.ppermute(part, axis, [(d, d ^ mask) for d in range(ways)])]
    all_to_all x1 -> x0, waiting for transfers between devices: 15.2 us -> none  [body(): lines = lax.all_to_all(flat, 'ax', split_axis=1, concat_axis=0, tiled=True)]
    all_to_all x1, waiting for transfers between devices: 23 us -> 11.8 us  [body(): lax.all_to_all(solved, 'ax', split_axis=1, concat_axis=2, tiled=True)]
    all_to_all x1 -> x0, starting transfers between devices: 7.22 us -> none  [body(): lines = lax.all_to_all(flat, 'ax', split_axis=1, concat_axis=0, tiled=True)]
    all_to_all x2 -> x0, local copies, waits for them, and re-layouts: 2.53 us -> none  [body(): lines = lax.all_to_all(flat, 'ax', split_axis=1, concat_axis=0, tiled=True)]
    all_to_all x1, starting transfers between devices: 4.77 us -> 7.26 us  [body(): lax.all_to_all(solved, 'ax', split_axis=1, concat_axis=2, tiled=True)]
    unnamed x5 -> x6, local copies, waits for them, and re-layouts: 0.07 us -> 1.55 us
  transfers between devices with their start and end apart: 4 -> 18, of which waited for: 3 -> 13; matrix products, arithmetic and copies ran while one was open for 6% -> 4% of each run, Pallas kernels for 0% -> 0%
where the time goes in v1:
time: 106 us; the launch traced here: 105 us
  starting transfers between devices  52.9 us (50%)
  waiting for transfers between devices  35 us (33%)
  local copies, waits for them, and re-layouts  8.09 us (8%)
  other arithmetic  4.76 us (4%)
  matrix products  2.53 us (2%)
  between operations  1.24 us (1%)
    ppermute x15, starting transfers between devices, pairwise_exchange(): part = lax.ppermute(part, axis, [(d, d ^ mask) for d in range(ways)])  41.4 us
    ppermute x15, waiting for transfers between devices, pairwise_exchange(): part = lax.ppermute(part, axis, [(d, d ^ mask) for d in range(ways)])  22.3 us
    all_to_all x1, waiting for transfers between devices, body(): lax.all_to_all(solved, 'ax', split_axis=1, concat_axis=2, tiled=True)  11.8 us
    all_to_all x1, starting transfers between devices, body(): lax.all_to_all(solved, 'ax', split_axis=1, concat_axis=2, tiled=True)  7.26 us
    ppermute x1, starting transfers between devices, with_halo(): before = lax.ppermute(last, axis, up)  3.05 us
  transfers between devices with their start and end apart: 18, of which 13 were waited for; matrix products, arithmetic and copies ran while one was open for 4% of the time, Pallas kernels for 0%

profile of v1, /device:TPU:8, one launch (start us, length us, event | category | flops | bytes accessed | tf_op | source)
XLA Modules:
  0.0 104.5 jit_solution(16231283856792833648)
XLA Ops:
  2.4 3.5 %collective-permute-start.14 = (f32[8,1280]{1,0:T(8,128)S(1)}, f32[8,1280]{1,0:T(8,128)S(1)}, u32[]{:S(2)}, u32[]{:S(2)}) collective-permute-start(f32[8,1280]{1,0:T(8,128)S(1)} %get-tuple-element.9), channel_id=1, source_target_pairs={{0,30},{2,28},{4,26},{6,24},{8,22},{10,20},{12,18},{14,16},{16,14}... | collective-permute-start | bytes 122888 | tf_op jit(solution)/shard_map/ppermute | solution.py:22
  13.9 2.4 %collective-permute-done.1 = f32[8,1280]{1,0:T(8,128)S(1)} collective-permute-done((f32[8,1280]{1,0:T(8,128)S(1)}, f32[8,1280]{1,0:T(8,128)S(1)}, u32[]{:S(2)}, u32[]{:S(2)}) %collective-permute-start.1) | collective-permute-done | bytes 40992 | tf_op jit(solution)/shard_map/ppermute | solution.py:22
  16.4 2.5 %collective-permute-start.2 = (f32[8,1280]{1,0:T(8,128)S(1)}, f32[8,1280]{1,0:T(8,128)S(1)}, u32[]{:S(2)}, u32[]{:S(2)}) collective-permute-start(f32[8,1280]{1,0:T(8,128)S(1)} %get-tuple-element.21), channel_id=1, source_target_pairs={{0,6},{2,4},{4,2},{6,0},{8,14},{10,12},{12,10},{14,8},{16,22},{18,... | collective-permute-start | bytes 122888 | tf_op jit(solution)/shard_map/ppermute | solution.py:22
  18.8 2.4 %collective-permute-done.2 = f32[8,1280]{1,0:T(8,128)S(1)} collective-permute-done((f32[8,1280]{1,0:T(8,128)S(1)}, f32[8,1280]{1,0:T(8,128)S(1)}, u32[]{:S(2)}, u32[]{:S(2)}) %collective-permute-start.2) | collective-permute-done | bytes 40992 | tf_op jit(solution)/shard_map/ppermute | solution.py:22
  21.3 4.0 %collective-permute-start.3 = (f32[8,1280]{1,0:T(8,128)S(1)}, f32[8,1280]{1,0:T(8,128)S(1)}, u32[]{:S(2)}, u32[]{:S(2)}) collective-permute-start(f32[8,1280]{1,0:T(8,128)S(1)} %get-tuple-element.20), channel_id=1, source_target_pairs={{0,8},{2,10},{4,12},{6,14},{8,0},{10,2},{12,4},{14,6},{16,24},{18,... | collective-permute-start | bytes 122888 | tf_op jit(solution)/shard_map/ppermute | solution.py:22
  25.3 2.0 %collective-permute-done.3 = f32[8,1280]{1,0:T(8,128)S(1)} collective-permute-done((f32[8,1280]{1,0:T(8,128)S(1)}, f32[8,1280]{1,0:T(8,128)S(1)}, u32[]{:S(2)}, u32[]{:S(2)}) %collective-permute-start.3) | collective-permute-done | bytes 40992 | tf_op jit(solution)/shard_map/ppermute | solution.py:22
  27.2 3.0 %collective-permute-start.4 = (f32[8,1280]{1,0:T(8,128)S(1)}, f32[8,1280]{1,0:T(8,128)S(1)}, u32[]{:S(2)}, u32[]{:S(2)}) collective-permute-start(f32[8,1280]{1,0:T(8,128)S(1)} %get-tuple-element.19), channel_id=1, source_target_pairs={{0,10},{2,8},{4,14},{6,12},{8,2},{10,0},{12,6},{14,4},{16,26},{18,... | collective-permute-start | bytes 122888 | tf_op jit(solution)/shard_map/ppermute | solution.py:22
  30.3 2.0 %collective-permute-done.4 = f32[8,1280]{1,0:T(8,128)S(1)} collective-permute-done((f32[8,1280]{1,0:T(8,128)S(1)}, f32[8,1280]{1,0:T(8,128)S(1)}, u32[]{:S(2)}, u32[]{:S(2)}) %collective-permute-start.4) | collective-permute-done | bytes 40992 | tf_op jit(solution)/shard_map/ppermute | solution.py:22
  32.2 3.0 %collective-permute-start.5 = (f32[8,1280]{1,0:T(8,128)S(1)}, f32[8,1280]{1,0:T(8,128)S(1)}, u32[]{:S(2)}, u32[]{:S(2)}) collective-permute-start(f32[8,1280]{1,0:T(8,128)S(1)} %get-tuple-element.18), channel_id=1, source_target_pairs={{0,12},{2,14},{4,8},{6,10},{8,4},{10,6},{12,0},{14,2},{16,28},{18,... | collective-permute-start | bytes 122888 | tf_op jit(solution)/shard_map/ppermute | solution.py:22
  35.2 2.0 %collective-permute-done.5 = f32[8,1280]{1,0:T(8,128)S(1)} collective-permute-done((f32[8,1280]{1,0:T(8,128)S(1)}, f32[8,1280]{1,0:T(8,128)S(1)}, u32[]{:S(2)}, u32[]{:S(2)}) %collective-permute-start.5) | collective-permute-done | bytes 40992 | tf_op jit(solution)/shard_map/ppermute | solution.py:22
  37.2 3.8 %collective-permute-start.6 = (f32[8,1280]{1,0:T(8,128)S(1)}, f32[8,1280]{1,0:T(8,128)S(1)}, u32[]{:S(2)}, u32[]{:S(2)}) collective-permute-start(f32[8,1280]{1,0:T(8,128)S(1)} %get-tuple-element.17), channel_id=1, source_target_pairs={{0,14},{2,12},{4,10},{6,8},{8,6},{10,4},{12,2},{14,0},{16,30},{18,... | collective-permute-start | bytes 122888 | tf_op jit(solution)/shard_map/ppermute | solution.py:22
  43.0 4.1 %collective-permute-start.7 = (f32[8,1280]{1,0:T(8,128)S(1)}, f32[8,1280]{1,0:T(8,128)S(1)}, u32[]{:S(2)}, u32[]{:S(2)}) collective-permute-start(f32[8,1280]{1,0:T(8,128)S(1)} %get-tuple-element.16), channel_id=1, source_target_pairs={{0,16},{2,18},{4,20},{6,22},{8,24},{10,26},{12,28},{14,30},{16,0},... | collective-permute-start | bytes 122888 | tf_op jit(solution)/shard_map/ppermute | solution.py:22
  47.1 2.4 %collective-permute-done.7 = f32[8,1280]{1,0:T(8,128)S(1)} collective-permute-done((f32[8,1280]{1,0:T(8,128)S(1)}, f32[8,1280]{1,0:T(8,128)S(1)}, u32[]{:S(2)}, u32[]{:S(2)}) %collective-permute-start.7) | collective-permute-done | bytes 40992 | tf_op jit(solution)/shard_map/ppermute | solution.py:22
  49.5 4.2 %collective-permute-start.8 = (f32[8,1280]{1,0:T(8,128)S(1)}, f32[8,1280]{1,0:T(8,128)S(1)}, u32[]{:S(2)}, u32[]{:S(2)}) collective-permute-start(f32[8,1280]{1,0:T(8,128)S(1)} %get-tuple-element.15), channel_id=1, source_target_pairs={{0,18},{2,16},{4,22},{6,20},{8,26},{10,24},{12,30},{14,28},{16,2},... | collective-permute-start | bytes 122888 | tf_op jit(solution)/shard_map/ppermute | solution.py:22
  53.7 2.0 %collective-permute-done.8 = f32[8,1280]{1,0:T(8,128)S(1)} collective-permute-done((f32[8,1280]{1,0:T(8,128)S(1)}, f32[8,1280]{1,0:T(8,128)S(1)}, u32[]{:S(2)}, u32[]{:S(2)}) %collective-permute-start.8) | collective-permute-done | bytes 40992 | tf_op jit(solution)/shard_map/ppermute | solution.py:22
  55.7 3.5 %collective-permute-start.9 = (f32[8,1280]{1,0:T(8,128)S(1)}, f32[8,1280]{1,0:T(8,128)S(1)}, u32[]{:S(2)}, u32[]{:S(2)}) collective-permute-start(f32[8,1280]{1,0:T(8,128)S(1)} %get-tuple-element.14), channel_id=1, source_target_pairs={{0,20},{2,22},{4,16},{6,18},{8,28},{10,30},{12,24},{14,26},{16,4},... | collective-permute-start | bytes 122888 | tf_op jit(solution)/shard_map/ppermute | solution.py:22
  59.2 2.3 %collective-permute-done.9 = f32[8,1280]{1,0:T(8,128)S(1)} collective-permute-done((f32[8,1280]{1,0:T(8,128)S(1)}, f32[8,1280]{1,0:T(8,128)S(1)}, u32[]{:S(2)}, u32[]{:S(2)}) %collective-permute-start.9) | collective-permute-done | bytes 40992 | tf_op jit(solution)/shard_map/ppermute | solution.py:22
  61.5 4.4 %collective-permute-start.10 = (f32[8,1280]{1,0:T(8,128)S(1)}, f32[8,1280]{1,0:T(8,128)S(1)}, u32[]{:S(2)}, u32[]{:S(2)}) collective-permute-start(f32[8,1280]{1,0:T(8,128)S(1)} %get-tuple-element.13), channel_id=1, source_target_pairs={{0,22},{2,20},{4,18},{6,16},{8,30},{10,28},{12,26},{14,24},{16,6},... | collective-permute-start | bytes 122888 | tf_op jit(solution)/shard_map/ppermute | solution.py:22
  65.9 2.3 %collective-permute-done.10 = f32[8,1280]{1,0:T(8,128)S(1)} collective-permute-done((f32[8,1280]{1,0:T(8,128)S(1)}, f32[8,1280]{1,0:T(8,128)S(1)}, u32[]{:S(2)}, u32[]{:S(2)}) %collective-permute-start.10) | collective-permute-done | bytes 40992 | tf_op jit(solution)/shard_map/ppermute | solution.py:22
  72.4 2.1 %copy.6 = f32[2,128,1280]{2,0,1:T(2,128)} copy(f32[2,128,1280]{2,1,0:T(8,128)S(1)} %bitcast.41) | data formatting | bytes 2621440 | tf_op jit(solution)/shard_map/reshape | solution.py:148
  74.5 7.3 %all-to-all-start = ((f32[2,128,1280]{2,0,1:T(2,128)}), f32[2,128,1280]{2,0,1:T(2,128)S(1)}, u32[]{:S(2)}, u32[]{:S(2)}) async-start(f32[2,128,1280]{2,0,1:T(2,128)} %copy.6), calls=%async_computation | async-start | bytes 2621440 | tf_op jit(solution)/shard_map/all_to_all | solution.py:149
  83.2 3.0 %collective-permute-start.16 = (f32[8,5,8,3]{3,2,1,0:T(8,128)S(1)}, f32[8,5,8,3]{3,2,1,0:T(8,128)S(1)}, u32[]{:S(2)}, u32[]{:S(2)}) collective-permute-start(f32[8,5,8,3]{3,2,1,0:T(8,128)S(1)} %get-tuple-element.6), channel_id=1, source_target_pairs={{0,1},{2,3},{4,5},{6,7},{8,9},{10,11},{12,13},{14,15},{16,17},{18,... | collective-permute-start | bytes 11528 | tf_op jit(solution)/shard_map/ppermute | solution.py:34
  87.2 2.0 %fusion.12 = f32[8,5,8,512]{3,2,1,0:T(8,128)} fusion(f32[8,5,8,512]{3,2,1,0:T(8,128)S(1)} %copy-done, f32[8,5,8,3]{3,2,1,0:T(8,128)S(1)} %collective-permute-done.16, f32[8,5,8,515]{3,2,1,0:T(8,128)S(1)} %constant_dynamic-update-slice_fusion.15), kind=kLoop, calls=%fused_computation.17 | loop fusion | flops 1802240 | bytes 3280640 | tf_op jit(solution)/shard_map/div | solution.py:135
  89.2 11.8 %all-to-all-done = f32[2,128,1280]{2,0,1:T(2,128)S(1)} async-done(((f32[2,128,1280]{2,0,1:T(2,128)}), f32[2,128,1280]{2,0,1:T(2,128)S(1)}, u32[]{:S(2)}, u32[]{:S(2)}) %all-to-all-start) | async-done | bytes 1310752 | tf_op jit(solution)/shard_map/all_to_all | solution.py:149
  (78 shorter events, 21.3 us)
Async XLA Ops:
  2.4 65.9 %collective-permute-start.14 = (f32[8,1280]{1,0:T(8,128)S(1)}, f32[8,1280]{1,0:T(8,128)S(1)}, u32[]{:S(2)}, u32[]{:S(2)}) collective-permute-start(f32[8,1280]{1,0:T(8,128)S(1)} %get-tuple-element.9), channel_id=1, source_target_pairs={{0,30},{2,28},{4,26},{6,24},{8,22},{10,20},{12,18},{14,16},{16,14}... | collective-permute-start | bytes 122888 | tf_op jit(solution)/shard_map/ppermute | solution.py:22
  6.0 62.3 %collective-permute-start.13 = (f32[8,1280]{1,0:T(8,128)S(1)}, f32[8,1280]{1,0:T(8,128)S(1)}, u32[]{:S(2)}, u32[]{:S(2)}) collective-permute-start(f32[8,1280]{1,0:T(8,128)S(1)} %get-tuple-element.10), channel_id=1, source_target_pairs={{0,28},{2,30},{4,24},{6,26},{8,20},{10,22},{12,16},{14,18},{16,12}... | collective-permute-start | bytes 122888 | tf_op jit(solution)/shard_map/ppermute | solution.py:22
  6.4 61.9 %collective-permute-start.12 = (f32[8,1280]{1,0:T(8,128)S(1)}, f32[8,1280]{1,0:T(8,128)S(1)}, u32[]{:S(2)}, u32[]{:S(2)}) collective-permute-start(f32[8,1280]{1,0:T(8,128)S(1)} %get-tuple-element.11), channel_id=1, source_target_pairs={{0,26},{2,24},{4,30},{6,28},{8,18},{10,16},{12,22},{14,20},{16,10}... | collective-permute-start | bytes 122888 | tf_op jit(solution)/shard_map/ppermute | solution.py:22
  7.9 60.3 %collective-permute-start.11 = (f32[8,1280]{1,0:T(8,128)S(1)}, f32[8,1280]{1,0:T(8,128)S(1)}, u32[]{:S(2)}, u32[]{:S(2)}) collective-permute-start(f32[8,1280]{1,0:T(8,128)S(1)} %get-tuple-element.12), channel_id=1, source_target_pairs={{0,24},{2,26},{4,28},{6,30},{8,16},{10,18},{12,20},{14,22},{16,8},... | collective-permute-start | bytes 122888 | tf_op jit(solution)/shard_map/ppermute | solution.py:22
  8.4 4.0 %collective-permute-start = (f32[8,1280]{1,0:T(8,128)S(1)}, f32[8,1280]{1,0:T(8,128)S(1)}, u32[]{:S(2)}, u32[]{:S(2)}) collective-permute-start(f32[8,1280]{1,0:T(8,128)S(1)} %get-tuple-element.23), channel_id=1, source_target_pairs={{0,2},{2,0},{4,6},{6,4},{8,10},{10,8},{12,14},{14,12},{16,18},{18,... | collective-permute-start | bytes 122888 | tf_op jit(solution)/shard_map/ppermute | solution.py:22
  12.4 4.0 %collective-permute-start.1 = (f32[8,1280]{1,0:T(8,128)S(1)}, f32[8,1280]{1,0:T(8,128)S(1)}, u32[]{:S(2)}, u32[]{:S(2)}) collective-permute-start(f32[8,1280]{1,0:T(8,128)S(1)} %get-tuple-element.22), channel_id=1, source_target_pairs={{0,4},{2,6},{4,0},{6,2},{8,12},{10,14},{12,8},{14,10},{16,20},{18,... | collective-permute-start | bytes 122888 | tf_op jit(solution)/shard_map/ppermute | solution.py:22
  16.4 4.9 %collective-permute-start.2 = (f32[8,1280]{1,0:T(8,128)S(1)}, f32[8,1280]{1,0:T(8,128)S(1)}, u32[]{:S(2)}, u32[]{:S(2)}) collective-permute-start(f32[8,1280]{1,0:T(8,128)S(1)} %get-tuple-element.21), channel_id=1, source_target_pairs={{0,6},{2,4},{4,2},{6,0},{8,14},{10,12},{12,10},{14,8},{16,22},{18,... | collective-permute-start | bytes 122888 | tf_op jit(solution)/shard_map/ppermute | solution.py:22
  21.3 6.0 %collective-permute-start.3 = (f32[8,1280]{1,0:T(8,128)S(1)}, f32[8,1280]{1,0:T(8,128)S(1)}, u32[]{:S(2)}, u32[]{:S(2)}) collective-permute-start(f32[8,1280]{1,0:T(8,128)S(1)} %get-tuple-element.20), channel_id=1, source_target_pairs={{0,8},{2,10},{4,12},{6,14},{8,0},{10,2},{12,4},{14,6},{16,24},{18,... | collective-permute-start | bytes 122888 | tf_op jit(solution)/shard_map/ppermute | solution.py:22
  27.2 5.0 %collective-permute-start.4 = (f32[8,1280]{1,0:T(8,128)S(1)}, f32[8,1280]{1,0:T(8,128)S(1)}, u32[]{:S(2)}, u32[]{:S(2)}) collective-permute-start(f32[8,1280]{1,0:T(8,128)S(1)} %get-tuple-element.19), channel_id=1, source_target_pairs={{0,10},{2,8},{4,14},{6,12},{8,2},{10,0},{12,6},{14,4},{16,26},{18,... | collective-permute-start | bytes 122888 | tf_op jit(solution)/shard_map/ppermute | solution.py:22
  32.2 4.9 %collective-permute-start.5 = (f32[8,1280]{1,0:T(8,128)S(1)}, f32[8,1280]{1,0:T(8,128)S(1)}, u32[]{:S(2)}, u32[]{:S(2)}) collective-permute-start(f32[8,1280]{1,0:T(8,128)S(1)} %get-tuple-element.18), channel_id=1, source_target_pairs={{0,12},{2,14},{4,8},{6,10},{8,4},{10,6},{12,0},{14,2},{16,28},{18,... | collective-permute-start | bytes 122888 | tf_op jit(solution)/shard_map/ppermute | solution.py:22
  37.2 5.8 %collective-permute-start.6 = (f32[8,1280]{1,0:T(8,128)S(1)}, f32[8,1280]{1,0:T(8,128)S(1)}, u32[]{:S(2)}, u32[]{:S(2)}) collective-permute-start(f32[8,1280]{1,0:T(8,128)S(1)} %get-tuple-element.17), channel_id=1, source_target_pairs={{0,14},{2,12},{4,10},{6,8},{8,6},{10,4},{12,2},{14,0},{16,30},{18,... | collective-permute-start | bytes 122888 | tf_op jit(solution)/shard_map/ppermute | solution.py:22
  43.0 6.5 %collective-permute-start.7 = (f32[8,1280]{1,0:T(8,128)S(1)}, f32[8,1280]{1,0:T(8,128)S(1)}, u32[]{:S(2)}, u32[]{:S(2)}) collective-permute-start(f32[8,1280]{1,0:T(8,128)S(1)} %get-tuple-element.16), channel_id=1, source_target_pairs={{0,16},{2,18},{4,20},{6,22},{8,24},{10,26},{12,28},{14,30},{16,0},... | collective-permute-start | bytes 122888 | tf_op jit(solution)/shard_map/ppermute | solution.py:22
  49.5 6.2 %collective-permute-start.8 = (f32[8,1280]{1,0:T(8,128)S(1)}, f32[8,1280]{1,0:T(8,128)S(1)}, u32[]{:S(2)}, u32[]{:S(2)}) collective-permute-start(f32[8,1280]{1,0:T(8,128)S(1)} %get-tuple-element.15), channel_id=1, source_target_pairs={{0,18},{2,16},{4,22},{6,20},{8,26},{10,24},{12,30},{14,28},{16,2},... | collective-permute-start | bytes 122888 | tf_op jit(solution)/shard_map/ppermute | solution.py:22
  55.7 5.8 %collective-permute-start.9 = (f32[8,1280]{1,0:T(8,128)S(1)}, f32[8,1280]{1,0:T(8,128)S(1)}, u32[]{:S(2)}, u32[]{:S(2)}) collective-permute-start(f32[8,1280]{1,0:T(8,128)S(1)} %get-tuple-element.14), channel_id=1, source_target_pairs={{0,20},{2,22},{4,16},{6,18},{8,28},{10,30},{12,24},{14,26},{16,4},... | collective-permute-start | bytes 122888 | tf_op jit(solution)/shard_map/ppermute | solution.py:22
  61.5 6.7 %collective-permute-start.10 = (f32[8,1280]{1,0:T(8,128)S(1)}, f32[8,1280]{1,0:T(8,128)S(1)}, u32[]{:S(2)}, u32[]{:S(2)}) collective-permute-start(f32[8,1280]{1,0:T(8,128)S(1)} %get-tuple-element.13), channel_id=1, source_target_pairs={{0,22},{2,20},{4,18},{6,16},{8,30},{10,28},{12,26},{14,24},{16,6},... | collective-permute-start | bytes 122888 | tf_op jit(solution)/shard_map/ppermute | solution.py:22
  74.5 7.3 %copy-start = (f32[8,5,8,512]{3,2,1,0:T(8,128)S(1)}, f32[8,5,8,512]{3,2,1,0:T(8,128)}, u32[]{:S(2)}) copy-start(f32[8,5,8,512]{3,2,1,0:T(8,128)} %param.1) | copy-start | bytes 1966084
  74.5 26.5 %all-to-all-start = ((f32[2,128,1280]{2,0,1:T(2,128)}), f32[2,128,1280]{2,0,1:T(2,128)S(1)}, u32[]{:S(2)}, u32[]{:S(2)}) async-start(f32[2,128,1280]{2,0,1:T(2,128)} %copy.6), calls=%async_computation | async-start | bytes 2621440 | tf_op jit(solution)/shard_map/all_to_all | solution.py:149
  81.9 4.4 %collective-permute-start.15 = (f32[8,5,8,3]{3,2,1,0:T(8,128)S(1)}, f32[8,5,8,3]{3,2,1,0:T(8,128)S(1)}, u32[]{:S(2)}, u32[]{:S(2)}) collective-permute-start(f32[8,5,8,3]{3,2,1,0:T(8,128)S(1)} %get-tuple-element.5), channel_id=1, source_target_pairs={{1,0},{3,2},{5,4},{7,6},{9,8},{11,10},{13,12},{15,14},{17,16},{19,... | collective-permute-start | bytes 11528 | tf_op jit(solution)/shard_map/ppermute | solution.py:35
  83.2 4.1 %collective-permute-start.16 = (f32[8,5,8,3]{3,2,1,0:T(8,128)S(1)}, f32[8,5,8,3]{3,2,1,0:T(8,128)S(1)}, u32[]{:S(2)}, u32[]{:S(2)}) collective-permute-start(f32[8,5,8,3]{3,2,1,0:T(8,128)S(1)} %get-tuple-element.6), channel_id=1, source_target_pairs={{0,1},{2,3},{4,5},{6,7},{8,9},{10,11},{12,13},{14,15},{16,17},{18,... | collective-permute-start | bytes 11528 | tf_op jit(solution)/shard_map/ppermute | solution.py:34
